TPU v7x, 32 devices: a whole 2x2x4 slice. The times are simulated.
32 devices in a mesh: slab: 2 (over y), frames: 4 (over z), medoids: 4 (over x, core).
Axes of the slice: x: 2, y: 2, z: 4, core: 2. Of those that a mesh axis runs over, the one named last changes fastest.
Arguments:
- frames: bfloat16 [16384, 512], P(('slab', 'frames')), parts along dimension 0, may hold values from -6 to 6
- medoids: bfloat16 [4, 8192, 512], P('medoids', 'frames'), may hold values from -6 to 6
- tile_ids: int32 [4, 128, 24], P('medoids', ('slab', 'frames')), parts along dimension 1, may hold values from 0 to 63, as said below
- tile_counts: int32 [4, 128], P('medoids', ('slab', 'frames')), parts along dimension 1, may hold values from 1 to 24, as said below
- plan: int32 [128], P('slab'), parts along dimension 0, may hold values from 0 to 63, as said below
Outputs:
- nearest: float32 [16384], P(('slab', 'frames')), parts along dimension 0
- second: float32 [16384], P(('slab', 'frames')), parts along dimension 0
There are 2 independent parts, one for each index of `slab`. A program takes and returns all parts, laid end to end along the dimension named above; an argument that names none is the same for every part. Nothing has to cross between parts.
Inputs may be any that keep to these rules, and one draw needn't show every extreme that they name: plan is a permutation. Of the frame tiles 16 i to 16 i + 15, at most 4 stand at positions 16 j to 16 j + 15 of plan's inverse for one j, and exactly 4 for some j, for every i. `tile_ids`: the 24 entries of one list are distinct; entries at l >= tile_counts[m, g] are ignored. `tile_counts`: the largest value is reached in every draw.
All inputs are finite; a program needn't handle non-finite values.
Results may differ from a plain program's by a relative error of at most 0.0003.
Values may be sent and summed in bfloat16 or wider, within the bound.
A program may use at most 64 MiB of HBM per device.

v0:
```python
import functools

import jax
import jax.numpy as jnp
from jax import lax
from jax.experimental import pallas as pl
from jax.experimental.pallas import tpu as pltpu
from jax.sharding import PartitionSpec as P

TILE = 128
BIG = 1e30
UNROLL = 4
LANES = 128
MESH = pl.DeviceIdType.MESH
F32 = jnp.float32


def remote(src, dst, send, recv, where):
    return pltpu.make_async_remote_copy(
        src_ref=src, dst_ref=dst, send_sem=send, recv_sem=recv, device_id=where, device_id_type=MESH
    )


def greet(targets):
    barrier = pltpu.get_barrier_semaphore()
    for where in targets:
        pl.semaphore_signal(barrier, inc=1, device_id=where, device_id_type=MESH)
    pl.semaphore_wait(barrier, len(targets))


def frame_gather_kernel(
    members, copies, parts, frames, meta, norm, medoids, out, all_frames, all_meta, all_norm,
    half_norm, penalty, best_one, best_two, own_sem, meta_send, meta_recv, norm_send, norm_recv,
    right_send, left_send, chain_recv, swap_send, swap_recv,
):
    me = lax.axis_index("frames")
    rep = lax.axis_index("medoids")
    blocks = frames.shape[0]
    share = blocks // copies
    piece = share // parts
    levels = copies.bit_length() - 1

    partners = []
    for level in range(levels):
        bit = copies >> (level + 1)
        partners.append((bit, {"medoids": rep + bit - 2 * bit * lax.rem(rep // bit, 2)}))
    others = [{"frames": lax.rem(me + k, members)} for k in range(1, members)]
    greet(others + [p[1] for p in partners])

    def place(block, owner_rep, part):
        return pl.ds(block * blocks + owner_rep * share + part * piece, piece)

    def chain(block, part, src, sends, to):
        return remote(
            src, all_frames.at[place(block, rep, part)], sends.at[block, part],
            chain_recv.at[block, part], {"frames": to},
        )

    def own_part(part):
        return frames.at[pl.ds(rep * share + part * piece, piece)]

    def held_part(block, part):
        return all_frames.at[place(block, rep, part)]

    own = pltpu.make_async_copy(frames, all_frames.at[pl.ds(me * blocks, blocks)], own_sem.at[0])
    own.start()
    own_meta = pltpu.make_async_copy(meta, all_meta.at[me], own_sem.at[1])
    own_meta.start()
    own_norm = pltpu.make_async_copy(norm, all_norm.at[me], own_sem.at[2])
    own_norm.start()
    small = []
    for k, where in enumerate(others):
        small.append(remote(meta, all_meta.at[me], meta_send.at[k], meta_recv.at[k], where))
        small.append(remote(norm, all_norm.at[me], norm_send.at[k], norm_recv.at[k], where))
    for copy in small:
        copy.start()

    for part in range(parts):
        @pl.when(me < members - 1)
        def _():
            chain(me, part, own_part(part), right_send, me + 1).start()

        @pl.when(me > 0)
        def _():
            chain(me, part, own_part(part), left_send, me - 1).start()

    def swap(block, part, level, index):
        holder = rep
        for earlier in range(level):
            if (index >> earlier) & 1:
                bit = partners[earlier][0]
                holder = holder + bit - 2 * bit * lax.rem(rep // bit, 2)
        slot = (1 << level) - 1 + index
        ref = all_frames.at[place(block, holder, part)]
        return remote(
            ref, ref, swap_send.at[block, part, slot], swap_recv.at[block, part, slot],
            partners[level][1],
        )

    def sides(step):
        return ((me - step >= 0, me - step, 0), (me + step <= members - 1, me + step, 1))

    def at_arrival(step, part):
        for exists, block, side in sides(step):
            @pl.when(exists)
            def _():
                chain(block, part, held_part(block, part), right_send, me).wait_recv()
                if side == 0:
                    @pl.when(me < members - 1)
                    def _():
                        chain(block, part, held_part(block, part), right_send, me + 1).start()
                else:
                    @pl.when(me > 0)
                    def _():
                        chain(block, part, held_part(block, part), left_send, me - 1).start()
                for level in range(levels):
                    swap(block, part, level, 0).start()

    def at_level(step, part, level):
        for exists, block, _side in sides(step):
            @pl.when(exists)
            def _():
                for index in range(1 << level):
                    swap(block, part, level, index).wait_recv()
                    mine = index | (1 << level)
                    for later in range(level + 1, levels):
                        swap(block, part, later, mine).start()

    units = [(step, part) for step in range(1, members) for part in range(parts)]
    held = medoids.shape[0]
    width = medoids.shape[2]
    rows = 8
    wide = 2 if blocks % 2 == 0 else 1
    deep = 4 if held % 4 == 0 else 1

    def half(index, carry):
        tile = medoids[index].astype(F32)
        total = jnp.sum(tile * tile, axis=1, keepdims=True) * 0.5
        half_norm[index] = jnp.broadcast_to(total, (TILE, TILE))
        return carry

    lax.fori_loop(0, held, half, 0)
    own.wait()
    own_meta.wait()
    own_norm.wait()
    for copy in small:
        copy.wait_send()
        copy.wait_recv()

    def compute(block):
        def some(index, carry):
            at = block * blocks + index * wide
            for k in range(wide):
                row = all_meta[block, pl.ds(index * wide + k, 1), :]
                penalty[k] = jnp.broadcast_to(row, (LANES, LANES)).T
            batch = all_frames[pl.ds(at, wide)].reshape(wide * TILE, width)
            best = [None] * wide
            for start in range(0, held, deep):
                inner = lax.dot_general(
                    medoids[start:start + deep].reshape(deep * TILE, width), batch,
                    (((1,), (1,)), ((), ())), preferred_element_type=F32,
                )
                for j in range(deep):
                    for k in range(wide):
                        value = half_norm[start + j] - inner[
                            j * TILE:(j + 1) * TILE, k * TILE:(k + 1) * TILE
                        ]
                        found = fold_rows(value, rows)
                        more = penalty[k, pl.ds(me * held + start + j, 1), :]
                        found = (found[0] + more, found[1] + more)
                        best[k] = found if best[k] is None else fold_two(*best[k], *found)
            for k in range(wide):
                best_one[at + k] = best[k][0]
                best_two[at + k] = best[k][1]
            return carry

        lax.fori_loop(0, blocks // wide, some, 0)

    compute(me)

    def finish(step):
        for level in range(levels):
            for part in range(parts):
                at_level(step, part, level)
        for exists, block, _side in sides(step):
            @pl.when(exists)
            def _():
                compute(block)

    for step in range(1, members):
        for part in range(parts):
            at_arrival(step, part)
            if part == 0 and step > 1:
                finish(step - 1)
    finish(members - 1)

    total = all_norm[...].reshape(members * blocks, TILE)
    one, two = best_one[:, 0, :], best_two[:, 0, :]
    for i in range(1, rows):
        one, two = fold_two(one, two, best_one[:, i, :], best_two[:, i, :])
    out[0] = (total + 2.0 * one) / width
    out[1] = (total + 2.0 * two) / width

    for part in range(parts):
        @pl.when(me < members - 1)
        def _():
            chain(me, part, own_part(part), right_send, me + 1).wait_send()

        @pl.when(me > 0)
        def _():
            chain(me, part, own_part(part), left_send, me - 1).wait_send()
    for step, part in units:
        for exists, block, side in sides(step):
            @pl.when(exists)
            def _():
                if side == 0:
                    @pl.when(me < members - 1)
                    def _():
                        chain(block, part, held_part(block, part), right_send, me + 1).wait_send()
                else:
                    @pl.when(me > 0)
                    def _():
                        chain(block, part, held_part(block, part), left_send, me - 1).wait_send()
                for level in range(levels):
                    for index in range(1 << level):
                        swap(block, part, level, index).wait_send()


def gather_frames(mesh, tiles, meta, norm, medoid_tiles):
    members, copies = mesh.shape["frames"], mesh.shape["medoids"]
    blocks = tiles.shape[0]
    share = blocks // copies
    parts = 2 if share % 2 == 0 else 1
    dma = pltpu.SemaphoreType.DMA
    hbm = pl.BlockSpec(memory_space=pl.ANY)
    vmem = pl.BlockSpec(memory_space=pltpu.VMEM)
    slots = max(copies - 1, 1)
    number, held = members * blocks, medoid_tiles.shape[0]
    return pl.pallas_call(
        functools.partial(frame_gather_kernel, members, copies, parts),
        out_shape=jax.ShapeDtypeStruct((2, number, TILE), F32),
        in_specs=[hbm, vmem, vmem, vmem],
        out_specs=vmem,
        scratch_shapes=[
            pltpu.VMEM((number,) + tiles.shape[1:], tiles.dtype),
            pltpu.VMEM((members,) + meta.shape, meta.dtype),
            pltpu.VMEM((members,) + norm.shape, norm.dtype),
            pltpu.VMEM((held, TILE, TILE), F32),
            pltpu.VMEM((2, LANES, LANES), F32),
            pltpu.VMEM((number, 8, TILE), F32),
            pltpu.VMEM((number, 8, TILE), F32),
            dma((3,)), dma((members,)), dma((members,)), dma((members,)), dma((members,)),
            dma((members, parts)), dma((members, parts)), dma((members, parts)),
            dma((members, parts, slots)), dma((members, parts, slots)),
        ],
        compiler_params=pltpu.CompilerParams(
            collective_id=0, has_side_effects=True, vmem_limit_bytes=44 * 1024 * 1024
        ),
        name="gather_frames",
    )(tiles, meta, norm, medoid_tiles)


def arrange_kernel(plan, part, out):
    def one(position, carry):
        for k in range(2):
            out[k, pl.ds(position, 1), :] = part[k, pl.ds(plan[position], 1), :]
        return carry

    lax.fori_loop(0, plan.shape[0], one, 0)


def arrange(plan, part):
    vmem = pl.BlockSpec(memory_space=pltpu.VMEM)
    return pl.pallas_call(
        arrange_kernel,
        out_shape=jax.ShapeDtypeStruct(part.shape, F32),
        in_specs=[pl.BlockSpec(memory_space=pltpu.SMEM), vmem],
        out_specs=vmem,
        name="arrange",
    )(plan, part)


def medoid_gather_kernel(members, part, whole, own_sem, send_sem, recv_sem):
    me = lax.axis_index("frames")
    count = part.shape[0]
    others = [{"frames": lax.rem(me + k, members)} for k in range(1, members)]
    if others:
        greet(others)
    mine = whole.at[pl.ds(me * count, count)]
    own = pltpu.make_async_copy(part, mine, own_sem)
    own.start()
    sent = [remote(part, mine, send_sem.at[k], recv_sem.at[k], w) for k, w in enumerate(others)]
    for copy in sent:
        copy.start()
    own.wait()
    for copy in sent:
        copy.wait_send()
        copy.wait_recv()


def gather_medoids(mesh, tiles):
    members = mesh.shape["frames"]
    dma = pltpu.SemaphoreType.DMA
    return pl.pallas_call(
        functools.partial(medoid_gather_kernel, members),
        out_shape=jax.ShapeDtypeStruct((members * tiles.shape[0],) + tiles.shape[1:], tiles.dtype),
        in_specs=[pl.BlockSpec(memory_space=pl.ANY)],
        out_specs=pl.BlockSpec(memory_space=pl.ANY),
        scratch_shapes=[dma, dma((members,)), dma((members,))],
        compiler_params=pltpu.CompilerParams(collective_id=1, has_side_effects=True),
        name="gather_medoids",
    )(tiles)


def fold_two(left_one, left_two, right_one, right_two):
    first = jnp.minimum(left_one, right_one)
    second = jnp.minimum(jnp.maximum(left_one, right_one), jnp.minimum(left_two, right_two))
    return first, second


def fold_rows(value, rows):
    chains = []
    for start in range(0, TILE, 4 * rows):
        parts = [value[start + i * rows:start + (i + 1) * rows] for i in range(4)]
        a, b = jnp.minimum(parts[0], parts[1]), jnp.maximum(parts[0], parts[1])
        c, d = jnp.minimum(parts[2], parts[3]), jnp.maximum(parts[2], parts[3])
        chains.append(fold_two(a, b, c, d))
    while len(chains) > 1:
        chains = [fold_two(*chains[i], *chains[i + 1]) for i in range(0, len(chains), 2)]
    return chains[0]


def pairs_kernel(
    longest, base, meta, plan, frames, norm, medoids, out,
    queue_frame, queue_medoid, half_norm, best_one, best_two, final_one, final_two,
):
    number = frames.shape[0]
    held = medoids.shape[0]
    width = frames.shape[2]
    rows = 8
    medoid_base, frame_base = base[0], base[1]

    def half(index, carry):
        tile = medoids[index].astype(F32)
        total = jnp.sum(tile * tile, axis=1, keepdims=True) * 0.5
        half_norm[index] = jnp.broadcast_to(total, (TILE, TILE))
        return carry

    lax.fori_loop(0, held, half, 0)

    def list_of(index, at):
        def entry(place, at):
            medoid = meta[index, place] - medoid_base
            queue_frame[at] = index
            queue_medoid[at] = medoid
            inside = jnp.logical_and(medoid >= 0, medoid < held)
            return at + inside.astype(jnp.int32)

        return lax.fori_loop(0, meta[index, longest], entry, at)

    length = lax.fori_loop(0, number, list_of, jnp.int32(0))
    for k in range(UNROLL):
        queue_frame[length + k] = number
        queue_medoid[length + k] = 0

    best_one[...] = jnp.full(best_one.shape, BIG, F32)
    best_two[...] = jnp.full(best_two.shape, BIG, F32)

    def work(step, carry):
        found = []
        for k in range(UNROLL):
            at = step * UNROLL + k
            row = queue_frame[at]
            medoid = queue_medoid[at]
            frame = jnp.minimum(row, number - 1)
            inner = lax.dot_general(
                medoids[medoid], frames[frame], (((1,), (1,)), ((), ())),
                preferred_element_type=F32,
            )
            value = half_norm[medoid] - inner
            chains = []
            for start in range(0, TILE, 4 * rows):
                parts = [value[start + i * rows:start + (i + 1) * rows] for i in range(4)]
                a, b = jnp.minimum(parts[0], parts[1]), jnp.maximum(parts[0], parts[1])
                c, d = jnp.minimum(parts[2], parts[3]), jnp.maximum(parts[2], parts[3])
                chains.append(fold_two(a, b, c, d))
            while len(chains) > 1:
                chains = [fold_two(*chains[i], *chains[i + 1]) for i in range(0, len(chains), 2)]
            found.append((row, chains[0]))
        for row, (one, two) in found:
            best_one[row], best_two[row] = fold_two(best_one[row], best_two[row], one, two)
        return carry

    lax.fori_loop(0, (length + UNROLL - 1) // UNROLL, work, 0)

    one, two = best_one[:number, 0, :], best_two[:number, 0, :]
    for i in range(1, rows):
        one, two = fold_two(one, two, best_one[:number, i, :], best_two[:number, i, :])
    final_one[...] = (norm[...] + 2.0 * one) / width
    final_two[...] = (norm[...] + 2.0 * two) / width

    def arrange(position, carry):
        source = plan[position] - frame_base
        mine = jnp.logical_and(source >= 0, source < number)
        row = jnp.clip(source, 0, number - 1)
        out[0, pl.ds(position, 1), :] = jnp.where(mine, final_one[pl.ds(row, 1), :], BIG)
        out[1, pl.ds(position, 1), :] = jnp.where(mine, final_two[pl.ds(row, 1), :], BIG)
        return carry

    lax.fori_loop(0, plan.shape[0], arrange, 0)


def pair_minima(base, meta, plan, tiles, norm, medoid_tiles, longest):
    number, held = tiles.shape[0], medoid_tiles.shape[0]
    smem = pl.BlockSpec(memory_space=pltpu.SMEM)
    vmem = pl.BlockSpec(memory_space=pltpu.VMEM)
    room = number * longest + 2 * UNROLL
    return pl.pallas_call(
        functools.partial(pairs_kernel, longest),
        out_shape=jax.ShapeDtypeStruct((2, plan.shape[0], TILE), F32),
        in_specs=[smem, smem, smem, vmem, vmem, vmem],
        out_specs=vmem,
        scratch_shapes=[
            pltpu.SMEM((room,), jnp.int32),
            pltpu.SMEM((room,), jnp.int32),
            pltpu.VMEM((held, TILE, TILE), F32),
            pltpu.VMEM((number + 1, 8, TILE), F32),
            pltpu.VMEM((number + 1, 8, TILE), F32),
            pltpu.VMEM((number, TILE), F32),
            pltpu.VMEM((number, TILE), F32),
        ],
        compiler_params=pltpu.CompilerParams(vmem_limit_bytes=40 * 1024 * 1024),
        name="pair_minima",
    )(base, meta, plan, tiles, norm, medoid_tiles)


def fold_kernel(
    members, groups, part, first, second, from_members, joined, from_groups,
    send_one, recv_one, send_two, recv_two,
):
    me = lax.axis_index("frames")
    group = lax.axis_index("medoids")
    blocks = first.shape[0]
    ways = [lax.rem(me + k, members) for k in range(1, members)]
    greet(
        [{"frames": w} for w in ways]
        + [{"medoids": lax.rem(group + k, groups)} for k in range(1, groups)]
    )
    copies = []
    for k, way in enumerate(ways):
        rows = pl.ds(pl.multiple_of(way * blocks, blocks), blocks)
        copies.append(
            remote(part.at[:, rows, :], from_members.at[k], send_one.at[k], recv_one.at[k], {"frames": way})
        )
    for copy in copies:
        copy.start()
    mine = pl.ds(pl.multiple_of(me * blocks, blocks), blocks)
    one, two = part[0, mine, :], part[1, mine, :]
    for k, copy in enumerate(copies):
        copy.wait_recv()
        one, two = fold_two(one, two, from_members[k, 0], from_members[k, 1])
    joined[0] = one
    joined[1] = two
    across = []
    for k in range(groups - 1):
        across.append(
            remote(
                joined, from_groups.at[k], send_two.at[k], recv_two.at[k],
                {"medoids": lax.rem(group + k + 1, groups)},
            )
        )
    for copy in across:
        copy.start()
    for k, copy in enumerate(across):
        copy.wait_recv()
        one, two = fold_two(one, two, from_groups[k, 0], from_groups[k, 1])
    first[...] = one
    second[...] = two
    for copy in copies + across:
        copy.wait_send()


def fold_everywhere(mesh, part, blocks):
    members, groups = mesh.shape["frames"], mesh.shape["medoids"]
    dma = pltpu.SemaphoreType.DMA
    vmem = pl.BlockSpec(memory_space=pltpu.VMEM)
    shape = jax.ShapeDtypeStruct((blocks, TILE), F32)
    return pl.pallas_call(
        functools.partial(fold_kernel, members, groups),
        out_shape=(shape, shape),
        in_specs=[vmem],
        out_specs=(vmem, vmem),
        scratch_shapes=[
            pltpu.VMEM((members, 2, blocks, TILE), F32),
            pltpu.VMEM((2, blocks, TILE), F32),
            pltpu.VMEM((groups, 2, blocks, TILE), F32),
            dma((members,)), dma((members,)), dma((groups,)), dma((groups,)),
        ],
        compiler_params=pltpu.CompilerParams(
            collective_id=2, has_side_effects=True, vmem_limit_bytes=40 * 1024 * 1024
        ),
        name="fold_everywhere",
    )(part)


def per_device(mesh, frames, medoids, tile_ids, tile_counts, plan):
    width = frames.shape[1]
    blocks = frames.shape[0] // TILE
    member = lax.axis_index("frames").astype(jnp.int32)
    members, copies = mesh.shape["frames"], mesh.shape["medoids"]
    longest = tile_ids.shape[2]
    tiles = frames.reshape(blocks, TILE, width)
    medoid_tiles = medoids[0].reshape(-1, TILE, width)
    norm = jnp.sum(jnp.square(frames.astype(F32)), axis=1).reshape(blocks, TILE)
    by_frames = (
        frames.shape[0] <= medoids.shape[1]
        and copies & (copies - 1) == 0
        and blocks % copies == 0
        and members > 1
        and members * medoid_tiles.shape[0] <= LANES
    )
    if by_frames:
        live = jnp.arange(longest)[None, :] < tile_counts[0][:, None]
        same = tile_ids[0][:, :, None] == jnp.arange(LANES)[None, None, :]
        listed = jnp.any(jnp.logical_and(live[:, :, None], same), axis=1)
        barred = jnp.where(listed, 0.0, BIG).astype(F32)
        part = arrange(plan, gather_frames(mesh, tiles, barred, norm, medoid_tiles))
    else:
        meta = jnp.concatenate([tile_ids[0], tile_counts[0][:, None]], axis=1)
        meta = jnp.pad(meta, ((0, 0), (0, LANES - longest - 1)))
        base = jnp.stack([jnp.int32(0), member * blocks])
        medoid_tiles = gather_medoids(mesh, medoid_tiles)
        part = pair_minima(base, meta, plan, tiles, norm, medoid_tiles, longest)
    first, second = fold_everywhere(mesh, part, blocks)
    return first.reshape(-1), second.reshape(-1)


def solution(mesh):
    placed = (
        P(("slab", "frames"), None),
        P("medoids", "frames", None),
        P("medoids", ("slab", "frames"), None),
        P("medoids", ("slab", "frames")),
        P("slab"),
    )
    return jax.shard_map(
        functools.partial(per_device, mesh),
        mesh=mesh,
        in_specs=placed,
        out_specs=(P(("slab", "frames")), P(("slab", "frames"))),
        check_vma=False,
    )
```

profile of v0, /device:TPU:0, one launch (start us, length us, event | category | flops | bytes accessed | tf_op | source)
XLA Modules:
  0.0 95.5 jit_solution(1493743051290231192)
XLA Ops:
  0.6 0.0 copy-start
  0.6 0.9 iota_compare_fusion.1
  1.5 0.9 fusion.1
  2.4 2.1 %multiply_reduce_fusion = f32[2048]{0:T(1024)S(1)} fusion(bf16[2048,512]{1,0:T(8,128)(2,1)} %param.5), kind=kLoop, calls=%fused_computation | loop fusion | flops 3143680 | bytes 2105344 | tf_op jit(solution)/shard_map/reduce_sum | solution.py:514
  4.5 0.0 copy-done
  4.5 0.0 copy-start.1
  4.5 1.6 %copy-done.1 = bf16[1,2048,512]{2,1,0:T(8,128)(2,1)S(1)} copy-done((bf16[1,2048,512]{2,1,0:T(8,128)(2,1)S(1)}, bf16[1,2048,512]{2,1,0:T(8,128)(2,1)}, u32[]{:S(2)}) %copy-start.1) | copy-done | bytes 2097176
  6.1 76.2 %gather_frames.1.part = f32[2,64,128]{2,1,0:T(8,128)S(1)} custom-call(bf16[16,128,512]{2,1,0:T(8,128)(2,1)S(1)} %bitcast.7, f32[16,128]{1,0:T(8,128)S(1)} %broadcast_select_fusion.meta, f32[16,128]{1,0:T(8,128)S(1)} %bitcast.9, bf16[16,128,512]{2,1,0:T(8,128)(2,1)S(1)} %bitcast.8), custom_call_target="tpu_custom_call" | custom-call | tf_op jit(solution)/shard_map/gather_frames/pallas_call | solution.py:239
  82.3 0.0 copy-start.2
  82.3 0.6 copy-done.2
  82.9 1.9 %arrange.1.part = f32[2,64,128]{2,1,0:T(8,128)} custom-call(s32[64]{0:T(128)} %plan.1, f32[2,64,128]{2,1,0:T(8,128)} %copy-done.2), custom_call_target="tpu_custom_call" | custom-call | tf_op jit(solution)/shard_map/arrange/pallas_call | solution.py:274
  84.8 0.0 copy-start.3
  84.8 0.8 copy-done.3
  85.6 8.7 %fold_everywhere.1 = (f32[16,128]{1,0:T(8,128)S(1)}, f32[16,128]{1,0:T(8,128)S(1)}) custom-call(f32[2,64,128]{2,1,0:T(8,128)S(1)} %copy-done.3), custom_call_target="tpu_custom_call" | custom-call | tf_op jit(solution)/shard_map/fold_everywhere/pallas_call | solution.py:488
  94.3 0.6 copy.9
  94.9 0.6 copy.10
  (1 shorter events, 0.0 us)
Async XLA Ops:
  0.6 3.9 %copy-start = (bf16[2048,512]{1,0:T(8,128)(2,1)S(1)}, bf16[2048,512]{1,0:T(8,128)(2,1)}, u32[]{:S(2)}) copy-start(bf16[2048,512]{1,0:T(8,128)(2,1)} %param.5) | copy-start | bytes 6291460
  4.5 1.6 %copy-start.1 = (bf16[1,2048,512]{2,1,0:T(8,128)(2,1)S(1)}, bf16[1,2048,512]{2,1,0:T(8,128)(2,1)}, u32[]{:S(2)}) copy-start(bf16[1,2048,512]{2,1,0:T(8,128)(2,1)} %param.6) | copy-start | bytes 6291460
  82.3 0.6 copy-start.2
  84.8 0.8 copy-start.3
where the time goes:
time: 95.8 us; the launch traced here: 95.5 us
  Pallas kernels  86.7 us (91%)
  local copies, waits for them, and re-layouts  4.24 us (4%)
  other arithmetic  3.83 us (4%)
    pallas_call x1, Pallas kernels, gather_frames(): pl.pallas_call(functools.partial(frame_gather_kernel, members, copies, pa...  76.2 us
    pallas_call x1, Pallas kernels, fold_everywhere(): pl.pallas_call(functools.partial(fold_kernel, members, groups), out_shape...  8.7 us
    unnamed x10, local copies, waits for them, and re-layouts  4.24 us
    reduce_sum x1, other arithmetic, per_device(): norm = jnp.sum(jnp.square(frames.astype(F32)), axis=1).reshape(blocks, TILE)  2.07 us

commit v1 on v0

--- a/solution.py
+++ b/solution.py
@@ -29,8 +29,8 @@
 
 
 def frame_gather_kernel(
-    members, copies, parts, frames, meta, norm, medoids, out, all_frames, all_meta, all_norm,
-    half_norm, penalty, best_one, best_two, own_sem, meta_send, meta_recv, norm_send, norm_recv,
+    members, copies, parts, frames, meta, medoids_far, out, all_frames, all_meta, all_norm,
+    medoids, norm, half_norm, penalty, best_one, best_two, own_sem, meta_send, meta_recv, norm_send, norm_recv,
     right_send, left_send, chain_recv, swap_send, swap_recv,
 ):
     me = lax.axis_index("frames")
@@ -66,12 +66,13 @@
     own.start()
     own_meta = pltpu.make_async_copy(meta, all_meta.at[me], own_sem.at[1])
     own_meta.start()
-    own_norm = pltpu.make_async_copy(norm, all_norm.at[me], own_sem.at[2])
-    own_norm.start()
+    fetch = pltpu.make_async_copy(medoids_far, medoids, own_sem.at[2])
+    fetch.start()
     small = []
+    norms = []
     for k, where in enumerate(others):
         small.append(remote(meta, all_meta.at[me], meta_send.at[k], meta_recv.at[k], where))
-        small.append(remote(norm, all_norm.at[me], norm_send.at[k], norm_recv.at[k], where))
+        norms.append(remote(norm, all_norm.at[me], norm_send.at[k], norm_recv.at[k], where))
     for copy in small:
         copy.start()
 
@@ -139,10 +140,16 @@
         half_norm[index] = jnp.broadcast_to(total, (TILE, TILE))
         return carry
 
+    own.wait()
+    for index in range(blocks):
+        tile = all_frames[me * blocks + index].astype(F32)
+        total = jnp.sum(tile * tile, axis=1, keepdims=True)
+        norm[index:index + 1, :] = jnp.broadcast_to(total, (TILE, TILE)).T[:1]
+    for copy in norms:
+        copy.start()
+    fetch.wait()
     lax.fori_loop(0, held, half, 0)
-    own.wait()
     own_meta.wait()
-    own_norm.wait()
     for copy in small:
         copy.wait_send()
         copy.wait_recv()
@@ -194,6 +201,10 @@
                 finish(step - 1)
     finish(members - 1)
 
+    for copy in norms:
+        copy.wait_send()
+        copy.wait_recv()
+    all_norm[me] = norm[...]
     total = all_norm[...].reshape(members * blocks, TILE)
     one, two = best_one[:, 0, :], best_two[:, 0, :]
     for i in range(1, rows):
@@ -226,7 +237,7 @@
                         swap(block, part, level, index).wait_send()
 
 
-def gather_frames(mesh, tiles, meta, norm, medoid_tiles):
+def gather_frames(mesh, tiles, meta, medoid_tiles):
     members, copies = mesh.shape["frames"], mesh.shape["medoids"]
     blocks = tiles.shape[0]
     share = blocks // copies
@@ -239,12 +250,14 @@
     return pl.pallas_call(
         functools.partial(frame_gather_kernel, members, copies, parts),
         out_shape=jax.ShapeDtypeStruct((2, number, TILE), F32),
-        in_specs=[hbm, vmem, vmem, vmem],
+        in_specs=[hbm, vmem, hbm],
         out_specs=vmem,
         scratch_shapes=[
             pltpu.VMEM((number,) + tiles.shape[1:], tiles.dtype),
             pltpu.VMEM((members,) + meta.shape, meta.dtype),
-            pltpu.VMEM((members,) + norm.shape, norm.dtype),
+            pltpu.VMEM((members, blocks, TILE), F32),
+            pltpu.VMEM(medoid_tiles.shape, medoid_tiles.dtype),
+            pltpu.VMEM((blocks, TILE), F32),
             pltpu.VMEM((held, TILE, TILE), F32),
             pltpu.VMEM((2, LANES, LANES), F32),
             pltpu.VMEM((number, 8, TILE), F32),
@@ -257,7 +270,7 @@
             collective_id=0, has_side_effects=True, vmem_limit_bytes=44 * 1024 * 1024
         ),
         name="gather_frames",
-    )(tiles, meta, norm, medoid_tiles)
+    )(tiles, meta, medoid_tiles)
 
 
 def arrange_kernel(plan, part, out):
@@ -511,7 +524,6 @@
     longest = tile_ids.shape[2]
     tiles = frames.reshape(blocks, TILE, width)
     medoid_tiles = medoids[0].reshape(-1, TILE, width)
-    norm = jnp.sum(jnp.square(frames.astype(F32)), axis=1).reshape(blocks, TILE)
     by_frames = (
         frames.shape[0] <= medoids.shape[1]
         and copies & (copies - 1) == 0
@@ -524,11 +536,12 @@
         same = tile_ids[0][:, :, None] == jnp.arange(LANES)[None, None, :]
         listed = jnp.any(jnp.logical_and(live[:, :, None], same), axis=1)
         barred = jnp.where(listed, 0.0, BIG).astype(F32)
-        part = arrange(plan, gather_frames(mesh, tiles, barred, norm, medoid_tiles))
+        part = arrange(plan, gather_frames(mesh, tiles, barred, medoid_tiles))
     else:
         meta = jnp.concatenate([tile_ids[0], tile_counts[0][:, None]], axis=1)
         meta = jnp.pad(meta, ((0, 0), (0, LANES - longest - 1)))
         base = jnp.stack([jnp.int32(0), member * blocks])
+        norm = jnp.sum(jnp.square(frames.astype(F32)), axis=1).reshape(blocks, TILE)
         medoid_tiles = gather_medoids(mesh, medoid_tiles)
         part = pair_minima(base, meta, plan, tiles, norm, medoid_tiles, longest)
     first, second = fold_everywhere(mesh, part, blocks)

time: 95.8 us -> 95.5 us (level)
  other arithmetic: 3.83 us -> 1.61 us
  local copies, waits for them, and re-layouts: 4.24 us -> 5.82 us
    reduce_sum x1 -> x0, other arithmetic: 2.07 us -> none  [per_device(): norm = jnp.sum(jnp.square(frames.astype(F32)), axis=1).reshape(blocks, TILE)]
    unnamed x10, local copies, waits for them, and re-layouts: 4.24 us -> 5.82 us
where the time goes in v1:
time: 95.5 us; the launch traced here: 95.2 us
  Pallas kernels  87.1 us (91%)
  local copies, waits for them, and re-layouts  5.82 us (6%)
  other arithmetic  1.61 us (2%)
    pallas_call x1, Pallas kernels, gather_frames(): pl.pallas_call(functools.partial(frame_gather_kernel, members, copies, pa...  76.4 us
    pallas_call x1, Pallas kernels, fold_everywhere(): pl.pallas_call(functools.partial(fold_kernel, members, groups), out_shape...  8.79 us
    unnamed x10, local copies, waits for them, and re-layouts  5.82 us

profile of v1, /device:TPU:0, one launch (start us, length us, event | category | flops | bytes accessed | tf_op | source)
XLA Modules:
  0.0 95.2 jit_solution(4353919285903019213)
XLA Ops:
  0.6 0.7 iota_compare_fusion.1
  1.4 0.9 fusion.1
  2.3 0.0 copy-start
  2.3 1.6 %copy-done = bf16[2048,512]{1,0:T(8,128)(2,1)S(1)} copy-done((bf16[2048,512]{1,0:T(8,128)(2,1)S(1)}, bf16[2048,512]{1,0:T(8,128)(2,1)}, u32[]{:S(2)}) %copy-start) | copy-done | bytes 2097176
  3.8 0.0 copy-start.1
  3.9 1.6 %copy-done.1 = bf16[1,2048,512]{2,1,0:T(8,128)(2,1)S(1)} copy-done((bf16[1,2048,512]{2,1,0:T(8,128)(2,1)S(1)}, bf16[1,2048,512]{2,1,0:T(8,128)(2,1)}, u32[]{:S(2)}) %copy-start.1) | copy-done | bytes 2097176
  5.4 76.4 %gather_frames.1.part = f32[2,64,128]{2,1,0:T(8,128)S(1)} custom-call(bf16[16,128,512]{2,1,0:T(8,128)(2,1)S(1)} %bitcast.6, f32[16,128]{1,0:T(8,128)S(1)} %broadcast_select_fusion.meta, bf16[16,128,512]{2,1,0:T(8,128)(2,1)S(1)} %bitcast.7), custom_call_target="tpu_custom_call" | custom-call | tf_op jit(solution)/shard_map/gather_frames/pallas_call | solution.py:250
  81.8 0.0 copy-start.2
  81.8 0.6 copy-done.2
  82.4 1.9 %arrange.1.part = f32[2,64,128]{2,1,0:T(8,128)} custom-call(s32[64]{0:T(128)} %plan.1, f32[2,64,128]{2,1,0:T(8,128)} %copy-done.2), custom_call_target="tpu_custom_call" | custom-call | tf_op jit(solution)/shard_map/arrange/pallas_call | solution.py:287
  84.3 0.0 copy-start.3
  84.3 0.8 copy-done.3
  85.2 8.8 %fold_everywhere.1 = (f32[16,128]{1,0:T(8,128)S(1)}, f32[16,128]{1,0:T(8,128)S(1)}) custom-call(f32[2,64,128]{2,1,0:T(8,128)S(1)} %copy-done.3), custom_call_target="tpu_custom_call" | custom-call | tf_op jit(solution)/shard_map/fold_everywhere/pallas_call | solution.py:501
  94.0 0.6 copy.9
  94.6 0.6 copy.10
  (1 shorter events, 0.0 us)
Async XLA Ops:
  2.3 1.6 %copy-start = (bf16[2048,512]{1,0:T(8,128)(2,1)S(1)}, bf16[2048,512]{1,0:T(8,128)(2,1)}, u32[]{:S(2)}) copy-start(bf16[2048,512]{1,0:T(8,128)(2,1)} %param.5) | copy-start | bytes 6291460
  3.8 1.6 %copy-start.1 = (bf16[1,2048,512]{2,1,0:T(8,128)(2,1)S(1)}, bf16[1,2048,512]{2,1,0:T(8,128)(2,1)}, u32[]{:S(2)}) copy-start(bf16[1,2048,512]{2,1,0:T(8,128)(2,1)} %param.6) | copy-start | bytes 6291460
  81.8 0.6 copy-start.2
  84.3 0.8 copy-start.3
